TPU v7x, 32 devices: a whole 2x2x4 slice. The times are simulated.
32 devices in a mesh: grp: 2 (over x), lon: 8 (over z, y), lat: 2 (over core).
Axes of the slice: x: 2, y: 2, z: 4, core: 2. Of those that a mesh axis runs over, the one named last changes fastest.
Arguments:
- right_side: float32 [8, 10, 64, 1024], P('grp', None, 'lat', 'lon'), parts along dimension 0, may hold values from -6 to 6
- kappa_sq: float32 [10, 64, 1024], P(None, 'lat', 'lon'), may hold values from 0.02 to 0.7
- flux_x: float32 [10, 64, 1024], P(None, 'lat', 'lon'), may hold values from 0.07 to 0.7
- flux_y: float32 [10, 64, 1024], P(None, 'lat', 'lon'), may hold values from 0.07 to 0.7
- flux_z: float32 [10, 64, 1024], P(None, 'lat', 'lon'), may hold values from 0.035 to 0.35
- wet_mask: int32 [10, 64, 1024], P(None, 'lat', 'lon'), may hold values from 0 to 1
- obs_cells: int32 [2, 8, 2048], P('lat', 'lon'), may hold values from 0 to 40959
- obs_weight: float32 [2, 8, 2048], P('lat', 'lon'), may hold values from 0.2 to 8
- obs_data: float32 [8, 2, 8, 2048], P('grp', 'lat', 'lon'), parts along dimension 0, may hold values from -6 to 6
Outputs:
- sample_field: float32 [8, 10, 64, 1024], P('grp', None, 'lat', 'lon'), parts along dimension 0
There are 2 independent parts, one for each index of `grp`. A program takes and returns all parts, laid end to end along the dimension named above; an argument that names none is the same for every part. Nothing has to cross between parts.
All inputs are finite; a program needn't handle non-finite values.
Results may differ from a plain program's by a relative error of at most 0.0001.
Values sent between devices are 32-bit elements; how exact they have to be, the bound alone decides.
A program may use at most 128 MiB of HBM per device.

v0:
```python
import jax
import jax.numpy as jnp
from jax import lax
from jax.sharding import PartitionSpec as P

ITERS = 2


def padded_2(block, sides, width):
    for axis, dim in sides:
        count = lax.axis_size(axis)
        forward = [(i, i + 1) for i in range(count - 1)]
        forward.append((count - 1, 0))
        backward = [(target, source) for source, target in forward]
        low = lax.ppermute(
            lax.slice_in_dim(block, block.shape[dim] - width, None, axis=dim), axis, forward
        )
        high = lax.ppermute(lax.slice_in_dim(block, 0, width, axis=dim), axis, backward)
        block = jnp.concatenate([low, block, high], axis=dim)
    return block


def center(field):
    return field[..., 1:-1, 1:-1]


def masked_pass(padded, coefs):
    kappa, hx_face, hy_face, hz_face, maskf = coefs
    masked = maskf * padded
    inner = center(masked)
    zconfig = [(0, 0)] * (inner.ndim - 3) + [(1, 1), (0, 0), (0, 0)]
    deeper = jnp.pad(inner, zconfig)
    hz_here = center(hz_face)
    hz_above = jnp.pad(hz_here, ((1, 0), (0, 0), (0, 0)))[:-1]
    total = center(kappa) * inner
    total = total + center(hx_face) * (inner - masked[..., 1:-1, 2:])
    total = total + hx_face[:, 1:-1, :-2] * (inner - masked[..., 1:-1, :-2])
    total = total + center(hy_face) * (inner - masked[..., 2:, 1:-1])
    total = total + hy_face[:, :-2, 1:-1] * (inner - masked[..., :-2, 1:-1])
    total = total + hz_here * (inner - deeper[..., 2:, :, :])
    total = total + hz_above * (inner - deeper[..., :-2, :, :])
    mask_inner = center(maskf)
    return mask_inner * total + (1.0 - mask_inner) * center(padded)


def precond_diag(coefs, obs_prec):
    kappa, hx_face, hy_face, hz_face, maskf = coefs
    hz_here = center(hz_face)
    hz_above = jnp.pad(hz_here, ((1, 0), (0, 0), (0, 0)))[:-1]
    diag_l = (
        center(kappa)
        + center(hx_face)
        + hx_face[:, 1:-1, :-2]
        + center(hy_face)
        + hy_face[:, :-2, 1:-1]
        + hz_here
        + hz_above
    )
    mask_inner = center(maskf)
    scaled = mask_inner * diag_l + (1.0 - mask_inner)
    return 1.0 / (scaled * scaled + obs_prec)


def clear_ends(padded, width):
    rows = jnp.arange(padded.shape[-2], dtype=jnp.int32)
    index = lax.axis_index("lat")
    last = lax.axis_size("lat") - 1
    lower = jnp.logical_and(index == 0, rows < width)
    upper = jnp.logical_and(index == last, rows >= padded.shape[-2] - width)
    keep = jnp.where(jnp.logical_or(lower, upper), 0.0, 1.0).astype(jnp.float32)
    return padded * keep[:, None]


def inner_sums(left, right):
    return jnp.sum(left * right, axis=(1, 2, 3))


def per_device(
    right_side, kappa_sq, flux_x, flux_y, flux_z, wet_mask, obs_cells, obs_weight, obs_data
):
    samples = right_side.shape[0]
    levels, rows_here, cols_here = kappa_sq.shape
    maskf = wet_mask.astype(jnp.float32)
    stacked = jnp.stack([kappa_sq, flux_x, flux_y, flux_z, maskf])
    padded_coefs = clear_ends(padded_2(stacked, (("lon", 3), ("lat", 2)), 1), 1)
    wide_coefs = tuple((padded_coefs[i] for i in range(5)))
    near_coefs = tuple((a for a in wide_coefs))
    cells = levels * rows_here * cols_here
    flat = obs_cells.reshape(-1)
    weights = obs_weight.reshape(-1)
    obs_prec = (
        jnp.zeros((cells,), jnp.float32).at[flat].add(weights).reshape(levels, rows_here, cols_here)
    )
    valued = weights[None, :] * obs_data.reshape(samples, -1)
    shift = (
        jnp.zeros((samples, cells), jnp.float32)
        .at[:, flat]
        .add(valued)
        .reshape(samples, levels, rows_here, cols_here)
    )
    rhs = right_side + shift
    prec = precond_diag(near_coefs, obs_prec)

    def single(field):
        padded = clear_ends(padded_2(field, (("lon", 3), ("lat", 2)), 1), 1)
        return masked_pass(padded, near_coefs)

    solution = jnp.zeros_like(rhs)
    resid = rhs

    def norm_sum(resid_now, zvec_now):
        return lax.psum(inner_sums(resid_now, zvec_now), ("lon", "lat"))

    zvec = prec * resid
    direction = zvec
    gamma = norm_sum(resid, zvec)
    for step in range(ITERS):
        image = single(single(direction)) + obs_prec * direction
        alpha = gamma / lax.psum(inner_sums(direction, image), ("lon", "lat"))
        solution = solution + alpha[:, None, None, None] * direction
        resid = resid - alpha[:, None, None, None] * image
        if step + 1 < ITERS:
            zvec = prec * resid
            gamma_new = norm_sum(resid, zvec)
            direction = zvec + (gamma_new / gamma)[:, None, None, None] * direction
            gamma = gamma_new
    return solution


def solution(mesh):
    return jax.shard_map(
        per_device,
        mesh=mesh,
        in_specs=(
            P("grp", None, "lat", "lon"),
            P(None, "lat", "lon"),
            P(None, "lat", "lon"),
            P(None, "lat", "lon"),
            P(None, "lat", "lon"),
            P(None, "lat", "lon"),
            P("lat", "lon", None),
            P("lat", "lon", None),
            P("grp", "lat", "lon", None),
        ),
        out_specs=P("grp", None, "lat", "lon"),
        check_vma=False,
    )
```

profile of v0, /device:TPU:0, one launch (start us, length us, event | category | flops | bytes accessed | tf_op | source)
XLA Modules:
  0.0 225.0 jit_solution(9877969289683836992)
XLA Ops:
  0.9 0.9 bitcast_dynamic-update-slice_fusion.3
  3.7 0.9 bitcast_dynamic-update-slice_fusion
  5.4 6.0 %collective-permute-start.1 = (f32[5,10,32,1]{2,3,1,0:T(1,128)S(1)}, f32[5,10,32,1]{2,3,1,0:T(1,128)S(1)}, u32[]{:S(2)}, u32[]{:S(2)}) collective-permute-start(f32[5,10,32,1]{2,3,1,0:T(1,128)S(1)} %copy.146), channel_id=1, source_target_pairs={{2,0},{4,2},{6,4},{8,6},{10,8},{12,10},{14,12},{0,14},{3,1},{5,3},... | collective-permute-start | bytes 19208 | tf_op jit(solution)/shard_map/ppermute | solution.py:18
  11.9 6.4 %collective-permute-done = f32[5,10,32,1]{2,3,1,0:T(1,128)S(1)} collective-permute-done((f32[5,10,32,1]{2,3,1,0:T(1,128)S(1)}, f32[5,10,32,1]{2,3,1,0:T(1,128)S(1)}, u32[]{:S(2)}, u32[]{:S(2)}) %collective-permute-start) | collective-permute-done | bytes 6432 | tf_op jit(solution)/shard_map/ppermute | solution.py:15
  20.1 1.4 copy.143
  21.4 11.3 %scatter_custom_fusion.1 = f32[40960]{0:T(1024)S(1)} fusion(s32[2048]{0:T(1024)S(1)} %bitcast.38, f32[2048]{0:T(1024)S(1)} %bitcast.37, f32[]{:T(128)} %constant.7.clone.1), kind=kCustom, calls=%fused_computation.129 | custom fusion | flops 2048 | bytes 163844 | tf_op jit(solution)/shard_map/scatter-add | solution.py:92
  32.7 20.1 %scatter_custom_fusion = f32[4,40960]{0,1:T(8,128)} fusion(s32[2048]{0:T(1024)S(1)} %bitcast.39, f32[2048,4]{1,0:T(8,128)} %copy.143, f32[]{:T(128)} %constant.7.clone.1), kind=kCustom, calls=%fused_computation.2 | custom fusion | flops 8192 | bytes 655872 | tf_op jit(solution)/shard_map/scatter-add | solution.py:98
  52.9 11.4 %copy.181 = f32[4,10,32,128]{3,2,1,0:T(8,128)S(1)} copy(f32[4,10,32,128]{0,3,2,1:T(8,128)} %bitcast.32) | data formatting | bytes 1310720 | tf_op jit(solution)/shard_map/reshape | solution.py:99
  65.5 1.4 fusion.80
  68.3 4.9 %collective-permute-start.5 = (f32[4,10,32,1]{2,1,3,0:T(8,128)S(1)}, f32[4,10,32,1]{2,1,3,0:T(8,128)}, u32[]{:S(2)}, u32[]{:S(2)}) collective-permute-start(f32[4,10,32,1]{2,1,3,0:T(8,128)S(1)} %copy.150), channel_id=1, source_target_pairs={{2,0},{4,2},{6,4},{8,6},{10,8},{12,10},{14,12},{0,14},{3,1},{5,3},... | collective-permute-start | bytes 15368 | tf_op jit(solution)/shard_map/ppermute | solution.py:18
  73.2 1.2 collective-permute-done.4
  74.8 1.1 copy.152
  81.2 5.2 %collective-permute-start.9 = (f32[4,10,32,1]{2,1,3,0:T(8,128)S(1)}, f32[4,10,32,1]{2,1,3,0:T(8,128)}, u32[]{:S(2)}, u32[]{:S(2)}) collective-permute-start(f32[4,10,32,1]{2,1,3,0:T(8,128)S(1)} %copy.158), channel_id=1, source_target_pairs={{2,0},{4,2},{6,4},{8,6},{10,8},{12,10},{14,12},{0,14},{3,1},{5,3},... | collective-permute-start | bytes 15368 | tf_op jit(solution)/shard_map/ppermute | solution.py:18
  86.3 1.4 collective-permute-done.8
  88.1 1.1 copy.160
  92.4 1.2 multiply_reduce_fusion
  93.6 34.4 %all-reduce.5 = (f32[4]{0:T(128)S(1)}, f32[4]{0:T(128)S(1)}) all-reduce(f32[4]{0:T(128)S(1)} %get-tuple-element.6, f32[4]{0:T(128)S(1)} %get-tuple-element.5), channel_id=1, replica_groups=mesh['grp'=2,'lon'=8,'lat'=2] {'lon','lat'}, use_global_device_ids=true, to_apply=%region_3.4 | all-reduce | flops 8 | bytes 64 | tf_op jit(solution)/shard_map/psum | solution.py:112
  128.3 29.5 %psum.30 = f32[4]{0:T(128)S(1)} all-reduce(f32[4]{0:T(128)S(1)} %fusion.37), channel_id=1, replica_groups=mesh['grp'=2,'lon'=8,'lat'=2] {'lon','lat'}, use_global_device_ids=true, to_apply=%region_7.8 | all-reduce | flops 4 | bytes 32 | tf_op jit(solution)/shard_map/psum | solution.py:112
  159.7 4.7 %collective-permute-start.13 = (f32[4,10,32,1]{2,1,3,0:T(8,128)S(1)}, f32[4,10,32,1]{2,1,3,0:T(8,128)}, u32[]{:S(2)}, u32[]{:S(2)}) collective-permute-start(f32[4,10,32,1]{2,1,3,0:T(8,128)S(1)} %copy.166), channel_id=1, source_target_pairs={{2,0},{4,2},{6,4},{8,6},{10,8},{12,10},{14,12},{0,14},{3,1},{5,3},... | collective-permute-start | bytes 15368 | tf_op jit(solution)/shard_map/ppermute | solution.py:18
  164.5 1.4 collective-permute-done.12
  166.2 1.1 copy.168
  171.4 1.1 fusion.76
  172.5 1.5 copy.173
  174.3 1.1 copy.174
  175.3 5.0 %collective-permute-start.17 = (f32[4,10,32,1]{2,1,3,0:T(8,128)}, f32[4,10,32,1]{2,1,3,0:T(8,128)}, u32[]{:S(2)}, u32[]{:S(2)}) collective-permute-start(f32[4,10,32,1]{2,1,3,0:T(8,128)} %copy.174), channel_id=1, source_target_pairs={{2,0},{4,2},{6,4},{8,6},{10,8},{12,10},{14,12},{0,14},{3,1},{5,3},... | collective-permute-start | bytes 15368 | tf_op jit(solution)/shard_map/ppermute | solution.py:18
  180.3 0.9 collective-permute-done.16
  181.2 1.1 copy.175
  182.3 1.9 copy.176
  184.2 1.4 pad_maximum_fusion.5
  188.6 1.1 fusion.70
  189.7 34.3 %psum.31 = f32[4]{0:T(128)S(1)} all-reduce(f32[4]{0:T(128)S(1)} %fusion.70), channel_id=1, replica_groups=mesh['grp'=2,'lon'=8,'lat'=2] {'lon','lat'}, use_global_device_ids=true, to_apply=%region_9.10 | all-reduce | flops 4 | bytes 32 | tf_op jit(solution)/shard_map/psum | solution.py:119
  224.0 1.0 multiply_add_fusion.1
  (182 shorter events, 26.7 us)
Async XLA Ops:
  5.0 6.9 %copy-start.33 = (f32[4,1,1,2048]{3,2,1,0:T(1,128)S(1)}, f32[4,1,1,2048]{3,2,1,0:T(1,128)}, u32[]{:S(2)}) copy-start(f32[4,1,1,2048]{3,2,1,0:T(1,128)} %param.17) | copy-start | bytes 98308
  5.0 6.9 %copy-start.39 = (f32[1,1,2048]{2,1,0:T(1,128)S(1)}, f32[1,1,2048]{2,1,0:T(1,128)}, u32[]{:S(2)}) copy-start(f32[1,1,2048]{2,1,0:T(1,128)} %param.16) | copy-start | bytes 24580
  5.0 6.9 %copy-start.40 = (s32[1,1,2048]{2,1,0:T(1,128)S(1)}, s32[1,1,2048]{2,1,0:T(1,128)}, u32[]{:S(2)}) copy-start(s32[1,1,2048]{2,1,0:T(1,128)} %param.15) | copy-start | bytes 24580
  5.4 13.4 %collective-permute-start.1 = (f32[5,10,32,1]{2,3,1,0:T(1,128)S(1)}, f32[5,10,32,1]{2,3,1,0:T(1,128)S(1)}, u32[]{:S(2)}, u32[]{:S(2)}) collective-permute-start(f32[5,10,32,1]{2,3,1,0:T(1,128)S(1)} %copy.146), channel_id=1, source_target_pairs={{2,0},{4,2},{6,4},{8,6},{10,8},{12,10},{14,12},{0,14},{3,1},{5,3},... | collective-permute-start | bytes 19208 | tf_op jit(solution)/shard_map/ppermute | solution.py:18
  11.8 6.6 %collective-permute-start = (f32[5,10,32,1]{2,3,1,0:T(1,128)S(1)}, f32[5,10,32,1]{2,3,1,0:T(1,128)S(1)}, u32[]{:S(2)}, u32[]{:S(2)}) collective-permute-start(f32[5,10,32,1]{2,3,1,0:T(1,128)S(1)} %copy.145), channel_id=1, source_target_pairs={{0,2},{2,4},{4,6},{6,8},{8,10},{10,12},{12,14},{14,0},{1,3},{3,5},... | collective-permute-start | bytes 19208 | tf_op jit(solution)/shard_map/ppermute | solution.py:15
  19.5 44.8 %collective-permute-start.2 = (f32[5,10,1,130]{3,2,1,0:T(1,128)S(1)}, f32[5,10,1,130]{3,2,1,0:T(1,128)S(1)}, u32[]{:S(2)}, u32[]{:S(2)}) collective-permute-start(f32[5,10,1,130]{3,2,1,0:T(1,128)S(1)} %get-tuple-element.20), channel_id=1, source_target_pairs={{0,1},{1,0},{2,3},{3,2},{4,5},{5,4},{6,7},{7,6},{8,9},{9,8},{10,11... | collective-permute-start | bytes 78008 | tf_op jit(solution)/shard_map/ppermute | solution.py:15
  19.6 44.7 %collective-permute-start.3 = (f32[5,10,1,130]{3,2,1,0:T(1,128)S(1)}, f32[5,10,1,130]{3,2,1,0:T(1,128)S(1)}, u32[]{:S(2)}, u32[]{:S(2)}) collective-permute-start(f32[5,10,1,130]{3,2,1,0:T(1,128)S(1)} %get-tuple-element.21), channel_id=1, source_target_pairs={{1,0},{0,1},{3,2},{2,3},{5,4},{4,5},{7,6},{6,7},{9,8},{8,9},{11,10... | collective-permute-start | bytes 78008 | tf_op jit(solution)/shard_map/ppermute | solution.py:18
  20.1 44.2 %copy-start.34 = (f32[34]{0:T(128)}, f32[34]{0:T(128)S(1)}, u32[]{:S(2)}) copy-start(f32[34]{0:T(128)S(1)} %or_select_fusion) | copy-start | bytes 412
  32.7 32.8 %copy-start.29 = (f32[40960]{0:T(1024)}, f32[40960]{0:T(1024)S(1)}, u32[]{:S(2)}) copy-start(f32[40960]{0:T(1024)S(1)} %scatter_custom_fusion.1) | copy-start | bytes 491524
  67.8 6.6 %collective-permute-start.4 = (f32[4,10,32,1]{2,1,3,0:T(8,128)S(1)}, f32[4,10,32,1]{2,1,3,0:T(8,128)S(1)}, u32[]{:S(2)}, u32[]{:S(2)}) collective-permute-start(f32[4,10,32,1]{2,1,3,0:T(8,128)S(1)} %copy.149), channel_id=1, source_target_pairs={{0,2},{2,4},{4,6},{6,8},{8,10},{10,12},{12,14},{14,0},{1,3},{3,5},... | collective-permute-start | bytes 15368 | tf_op jit(solution)/shard_map/ppermute | solution.py:15
  68.3 6.5 %collective-permute-start.5 = (f32[4,10,32,1]{2,1,3,0:T(8,128)S(1)}, f32[4,10,32,1]{2,1,3,0:T(8,128)}, u32[]{:S(2)}, u32[]{:S(2)}) collective-permute-start(f32[4,10,32,1]{2,1,3,0:T(8,128)S(1)} %copy.150), channel_id=1, source_target_pairs={{2,0},{4,2},{6,4},{8,6},{10,8},{12,10},{14,12},{0,14},{3,1},{5,3},... | collective-permute-start | bytes 15368 | tf_op jit(solution)/shard_map/ppermute | solution.py:18
  74.7 3.0 %copy-start.35 = (f32[34]{0:T(128)S(1)}, f32[34]{0:T(128)}, u32[]{:S(2)}) copy-start(f32[34]{0:T(128)} %copy-done.34) | copy-start | bytes 412
  76.2 1.3 collective-permute-start.7
  76.3 1.4 collective-permute-start.6
  80.7 7.1 %collective-permute-start.8 = (f32[4,10,32,1]{2,1,3,0:T(8,128)S(1)}, f32[4,10,32,1]{2,1,3,0:T(8,128)S(1)}, u32[]{:S(2)}, u32[]{:S(2)}) collective-permute-start(f32[4,10,32,1]{2,1,3,0:T(8,128)S(1)} %copy.157), channel_id=1, source_target_pairs={{0,2},{2,4},{4,6},{6,8},{8,10},{10,12},{12,14},{14,0},{1,3},{3,5},... | collective-permute-start | bytes 15368 | tf_op jit(solution)/shard_map/ppermute | solution.py:15
  81.2 6.9 %collective-permute-start.9 = (f32[4,10,32,1]{2,1,3,0:T(8,128)S(1)}, f32[4,10,32,1]{2,1,3,0:T(8,128)}, u32[]{:S(2)}, u32[]{:S(2)}) collective-permute-start(f32[4,10,32,1]{2,1,3,0:T(8,128)S(1)} %copy.158), channel_id=1, source_target_pairs={{2,0},{4,2},{6,4},{8,6},{10,8},{12,10},{14,12},{0,14},{3,1},{5,3},... | collective-permute-start | bytes 15368 | tf_op jit(solution)/shard_map/ppermute | solution.py:18
  88.0 3.0 %copy-start.36 = (f32[34]{0:T(128)S(1)}, f32[34]{0:T(128)}, u32[]{:S(2)}) copy-start(f32[34]{0:T(128)} %copy-done.34) | copy-start | bytes 412
  89.5 1.3 collective-permute-start.11
  89.6 1.4 collective-permute-start.10
  128.0 30.3 %copy-start.41 = (f32[4]{0:T(128)}, f32[4]{0:T(128)S(1)}, u32[]{:S(2)}) copy-start(f32[4]{0:T(128)S(1)} %div.13) | copy-start | bytes 52
  159.2 6.6 %collective-permute-start.12 = (f32[4,10,32,1]{2,1,3,0:T(8,128)S(1)}, f32[4,10,32,1]{2,1,3,0:T(8,128)S(1)}, u32[]{:S(2)}, u32[]{:S(2)}) collective-permute-start(f32[4,10,32,1]{2,1,3,0:T(8,128)S(1)} %copy.165), channel_id=1, source_target_pairs={{0,2},{2,4},{4,6},{6,8},{8,10},{10,12},{12,14},{14,0},{1,3},{3,5},... | collective-permute-start | bytes 15368 | tf_op jit(solution)/shard_map/ppermute | solution.py:15
  159.7 6.5 %collective-permute-start.13 = (f32[4,10,32,1]{2,1,3,0:T(8,128)S(1)}, f32[4,10,32,1]{2,1,3,0:T(8,128)}, u32[]{:S(2)}, u32[]{:S(2)}) collective-permute-start(f32[4,10,32,1]{2,1,3,0:T(8,128)S(1)} %copy.166), channel_id=1, source_target_pairs={{2,0},{4,2},{6,4},{8,6},{10,8},{12,10},{14,12},{0,14},{3,1},{5,3},... | collective-permute-start | bytes 15368 | tf_op jit(solution)/shard_map/ppermute | solution.py:18
  166.2 3.0 %copy-start.37 = (f32[34]{0:T(128)S(1)}, f32[34]{0:T(128)}, u32[]{:S(2)}) copy-start(f32[34]{0:T(128)} %copy-done.34) | copy-start | bytes 412
  167.6 1.3 collective-permute-start.15
  167.7 1.4 collective-permute-start.14
  174.0 7.2 %collective-permute-start.16 = (f32[4,10,32,1]{2,1,3,0:T(8,128)S(1)}, f32[4,10,32,1]{2,1,3,0:T(8,128)}, u32[]{:S(2)}, u32[]{:S(2)}) collective-permute-start(f32[4,10,32,1]{2,1,3,0:T(8,128)S(1)} %copy.173), channel_id=1, source_target_pairs={{0,2},{2,4},{4,6},{6,8},{8,10},{10,12},{12,14},{14,0},{1,3},{3,5},... | collective-permute-start | bytes 15368 | tf_op jit(solution)/shard_map/ppermute | solution.py:15
  175.3 7.0 %collective-permute-start.17 = (f32[4,10,32,1]{2,1,3,0:T(8,128)}, f32[4,10,32,1]{2,1,3,0:T(8,128)}, u32[]{:S(2)}, u32[]{:S(2)}) collective-permute-start(f32[4,10,32,1]{2,1,3,0:T(8,128)} %copy.174), channel_id=1, source_target_pairs={{2,0},{4,2},{6,4},{8,6},{10,8},{12,10},{14,12},{0,14},{3,1},{5,3},... | collective-permute-start | bytes 15368 | tf_op jit(solution)/shard_map/ppermute | solution.py:18
  182.3 4.9 %copy-start.38 = (f32[34]{0:T(128)S(1)}, f32[34]{0:T(128)}, u32[]{:S(2)}) copy-start(f32[34]{0:T(128)} %copy-done.34) | copy-start | bytes 412
  185.6 1.3 collective-permute-start.19
  185.7 1.4 collective-permute-start.18
  188.6 35.4 %copy-start.44 = (f32[4]{0:T(128)S(1)}, f32[4]{0:T(128)}, u32[]{:S(2)}) copy-start(f32[4]{0:T(128)} %copy-done.43) | copy-start | bytes 52
  188.6 35.4 %copy-start.42 = (f32[4]{0:T(128)S(1)}, f32[4]{0:T(128)}, u32[]{:S(2)}) copy-start(f32[4]{0:T(128)} %copy-done.41) | copy-start | bytes 52
  (33 other events, 41.8 us)
where the time goes:
time: 226 us; the launch traced here: 225 us
  blocking collectives  98.2 us (43%)
  other arithmetic  46.5 us (21%)
  local copies, waits for them, and re-layouts  35.5 us (16%)
  starting transfers between devices  29.1 us (13%)
  waiting for transfers between devices  14.9 us (7%)
    psum x2, blocking collectives, norm_sum(): return lax.psum(inner_sums(resid_now, zvec_now), ('lon', 'lat'))  63.9 us
    psum x1, blocking collectives, per_device(): alpha = gamma / lax.psum(inner_sums(direction, image), ('lon', 'lat'))  34.3 us
    ppermute x10, starting transfers between devices, padded_2(): lax.ppermute(lax.slice_in_dim(block, 0, width, axis=dim), axis, backward)  26.6 us
    scatter-add x1, other arithmetic, per_device(): shift = jnp.zeros((samples, cells), jnp.float32).at[:, flat].add(valued)....  20.1 us
    ppermute x10, waiting for transfers between devices, padded_2(): lax.ppermute(lax.slice_in_dim(block, block.shape[dim] - width, None, axis...  11.9 us
    reshape x1, local copies, waits for them, and re-layouts, per_device(): shift = jnp.zeros((samples, cells), jnp.float32).at[:, flat].add(valued)....  11.4 us
    scatter-add x1, other arithmetic, per_device(): jnp.zeros((cells,), jnp.float32).at[flat].add(weights)  11.3 us
    ppermute x9, local copies, waits for them, and re-layouts, padded_2(): lax.ppermute(lax.slice_in_dim(block, 0, width, axis=dim), axis, backward)  5.66 us
  transfers between devices with their start and end apart: 20, of which 13 were waited for; matrix products, arithmetic and copies ran while one was open for 22% of the time, Pallas kernels for 0%

commit v1 on v0

v1 whole, which is shorter than its diff:
```python
import functools

import jax
import jax.numpy as jnp
from jax import lax
from jax.experimental import pallas as pl
from jax.experimental.pallas import tpu as pltpu
from jax.sharding import PartitionSpec as P

MESH = pl.DeviceIdType.MESH
PAD = 8
F32 = jnp.float32


def kernel(
    n_lon, rs_ref, ka_ref, fx_ref, fy_ref, fz_ref, wm_ref, oc_ref, ow_ref, od_ref, out_ref,
    row_hot, bs, ops, prec, dg, cx, cxl, cy, cyu, cz, fa, fb, ww,
    col_send, col_recv, row_send, row_recv, part, slots, tot,
    send_sem, recv_sem, red_send, red_recv,
):
    samples, levels, rows, cols = rs_ref.shape
    blocks = rows // 8
    high = rows + 2 * PAD
    per_level = samples * blocks
    per_vreg = cols // per_level
    grp, lon, lat = lax.axis_index("grp"), lax.axis_index("lon"), lax.axis_index("lat")
    right = lax.rem(lon + 1, n_lon)
    left = lax.rem(lon + n_lon - 1, n_lon)
    group = 2 * n_lon
    me = lon * 2 + lat

    def peer(step):
        other = lax.rem(me + step, group)
        return (grp, other // 2, lax.rem(other, 2))

    barrier = pltpu.get_barrier_semaphore()
    for step in range(1, group):
        pl.semaphore_signal(barrier, inc=1, device_id=peer(step), device_id_type=MESH)

    is_low = lat == 0
    lane1 = lax.broadcasted_iota(jnp.int32, (8, cols), 1)
    lane32 = lax.broadcasted_iota(jnp.int32, (rows, cols), 1)
    row32 = lax.broadcasted_iota(jnp.int32, (rows, cols), 0)
    first_lane, last_lane = lane32 == 0, lane32 == cols - 1
    edge = jnp.where(is_low, rows - 1, 0)

    def exchange(slot):
        copies = []
        for side, target in ((0, (grp, right, lat)), (1, (grp, left, lat))):
            copies.append(pltpu.make_async_remote_copy(
                src_ref=col_send.at[slot, side], dst_ref=col_recv.at[slot, side],
                send_sem=send_sem.at[slot, side], recv_sem=recv_sem.at[slot, side],
                device_id=target, device_id_type=MESH))
        copies.append(pltpu.make_async_remote_copy(
            src_ref=row_send.at[slot], dst_ref=row_recv.at[slot],
            send_sem=send_sem.at[slot, 2], recv_sem=recv_sem.at[slot, 2],
            device_id=(grp, lon, 1 - lat), device_id_type=MESH))
        for copy in copies:
            copy.start()
        return copies

    def reduce_start(which):
        copies = []
        for step in range(1, group):
            copies.append(pltpu.make_async_remote_copy(
                src_ref=part.at[which], dst_ref=slots.at[which, step - 1],
                send_sem=red_send.at[which, step - 1], recv_sem=red_recv.at[which, step - 1],
                device_id=peer(step), device_id_type=MESH))
        for copy in copies:
            copy.start()
        return copies

    def reduce_finish(which, copies):
        total = part[which]
        for step, copy in enumerate(copies):
            copy.wait()
            total = total + slots[which, step]
        tot[which] = jnp.broadcast_to(jnp.sum(total, axis=1, keepdims=True), total.shape)

    to_right = jnp.zeros((8, cols), F32)
    to_left = jnp.zeros((8, cols), F32)
    for z in range(levels):
        for y in range(blocks):
            at = z * blocks + y
            here = pl.ds(y * 8, 8)
            flux = fx_ref[z, here, :]
            mask = wm_ref[z, here, :].astype(F32)
            to_right = jnp.where(lane1 == at, flux[:, cols - 1:cols], to_right)
            to_right = jnp.where(lane1 == at + cols // 2, mask[:, cols - 1:cols], to_right)
            to_left = jnp.where(lane1 == at, mask[:, 0:1], to_left)
    col_send[0, 0, 0] = to_right
    col_send[0, 1, 0] = to_left
    col_send[0, 0, 1] = jnp.zeros((8, cols), F32)
    col_send[0, 1, 1] = jnp.zeros((8, cols), F32)
    row_send[0] = jnp.zeros(row_send.shape[1:], F32)
    for z in range(levels):
        row_send[0, z:z + 1, :] = jnp.where(is_low, fy_ref[z, rows - 1:rows, :], fy_ref[z, 0:1, :])
        row_send[0, levels + z:levels + z + 1, :] = jnp.where(
            is_low, wm_ref[z, rows - 1:rows, :], wm_ref[z, 0:1, :]).astype(F32)

    pl.semaphore_wait(barrier, group - 1)
    copies = exchange(0)

    count = oc_ref.shape[-1]
    cells = oc_ref[0]
    flat_rows = levels * rows
    hot = lax.broadcasted_iota(jnp.int32, (flat_rows, count), 0) == cells // cols
    row_hot[...] = jnp.where(hot, 1.0, 0.0).astype(jnp.bfloat16)
    lane_hot = lax.broadcasted_iota(jnp.int32, (cols, count), 0) == lax.rem(cells, cols)
    weight = ow_ref[0]

    def scatter(value):
        top = value.astype(jnp.bfloat16).astype(F32)
        low = value - top
        both = jnp.concatenate(
            [jnp.where(lane_hot, top, 0.0), jnp.where(lane_hot, low, 0.0)], axis=0
        ).astype(jnp.bfloat16)
        got = lax.dot_general(
            row_hot[...], both, (((1,), (1,)), ((), ())), preferred_element_type=F32)
        return (got[:, :cols] + got[:, cols:]).reshape(levels, rows, cols)

    ops[...] = scatter(weight)
    for k in range(samples):
        bs[k] = rs_ref[k] + scatter(weight * od_ref[k, 0])

    for copy in copies:
        copy.wait()

    from_left, from_right = col_recv[0, 0, 0], col_recv[0, 1, 0]

    def column(packed, at):
        return jnp.concatenate(
            [jnp.broadcast_to(packed[:, at + y:at + y + 1], (8, cols)) for y in range(blocks)],
            axis=0)

    above = jnp.zeros((rows, cols), F32)
    for z in range(levels):
        mask = wm_ref[z].astype(F32)
        flux_x, flux_y, flux_z = fx_ref[z], fy_ref[z], fz_ref[z]
        at = z * blocks
        fx_left = jnp.where(first_lane, column(from_left, at), pltpu.roll(flux_x, 1, 1))
        m_left = jnp.where(first_lane, column(from_left, at + cols // 2), pltpu.roll(mask, 1, 1))
        m_right = jnp.where(last_lane, column(from_right, at), pltpu.roll(mask, cols - 1, 1))
        halo_fy = row_recv[0, z:z + 1, :]
        halo_m = row_recv[0, levels + z:levels + z + 1, :]
        fy_up = jnp.where(row32 == 0, jnp.where(is_low, 0.0, halo_fy), pltpu.roll(flux_y, 1, 0))
        m_up = jnp.where(row32 == 0, jnp.where(is_low, 0.0, halo_m), pltpu.roll(mask, 1, 0))
        m_down = jnp.where(
            row32 == rows - 1, jnp.where(is_low, halo_m, 0.0), pltpu.roll(mask, rows - 1, 0))
        diag = ka_ref[z] + flux_x + fx_left + flux_y + fy_up + flux_z + above
        scaled = mask * diag + (1.0 - mask)
        dg[z] = scaled
        prec[z] = 1.0 / (scaled * scaled + ops[z])
        cx[z] = flux_x * mask * m_right
        cxl[z] = fx_left * mask * m_left
        cy[z] = flux_y * mask * m_down
        cyu[z] = fy_up * mask * m_up
        if z + 1 < levels:
            cz[z] = flux_z * mask * wm_ref[z + 1].astype(F32)
        above = flux_z

    def base(k, z):
        return (k * levels + z) * high

    group_lane = lax.broadcasted_iota(jnp.int32, (per_level, 8, cols), 2) - lax.broadcasted_iota(
        jnp.int32, (per_level, 8, cols), 0)

    class Packer:
        def __init__(self):
            self.acc = [[jnp.zeros((8, cols), F32)] * 2 for _ in range(2)]

        def add(self, z, values):
            half, at = z // per_vreg, (z % per_vreg) * per_level
            tiles = jnp.stack(values).reshape(per_level, 8, cols)
            here = group_lane == at
            for side, lane in ((0, cols - 1), (1, 0)):
                edge_col = jnp.broadcast_to(tiles[:, :, lane:lane + 1], tiles.shape)
                self.acc[side][half] = self.acc[side][half] + jnp.sum(
                    jnp.where(here, edge_col, 0.0), axis=0)

        def send(self, slot, field):
            for side in range(2):
                for half in range(2):
                    col_send[slot, side, half] = self.acc[side][half]
            low = field[pl.ds(PAD, samples * levels, stride=high), :]
            top = field[pl.ds(PAD + rows - 1, samples * levels, stride=high), :]
            row_send[slot] = jnp.where(is_low, top, low)
            return exchange(slot)

    def put_rows(slot, field):
        got = row_recv[slot]
        field[pl.ds(PAD - 1, samples * levels, stride=high), :] = jnp.where(is_low, 0.0, got)
        field[pl.ds(PAD + rows, samples * levels, stride=high), :] = jnp.where(is_low, got, 0.0)

    def apply(slot, field, k, z, packs):
        at = base(k, z) + PAD
        here = field[pl.ds(at, rows), :]
        up = field[pl.ds(at - 1, rows), :]
        down = field[pl.ds(at + 1, rows), :]
        half, lane = z // per_vreg, (z % per_vreg) * per_level + k * blocks
        west = jnp.where(first_lane, column(packs[0][half], lane), pltpu.roll(here, 1, 1))
        east = jnp.where(last_lane, column(packs[1][half], lane), pltpu.roll(here, cols - 1, 1))
        total = dg[z] * here - cx[z] * east - cxl[z] * west - cy[z] * down - cyu[z] * up
        if z > 0:
            total = total - cz[z - 1] * field[pl.ds(at - high, rows), :]
        if z + 1 < levels:
            total = total - cz[z] * field[pl.ds(at + high, rows), :]
        return here, total

    def received(slot):
        return [[col_recv[slot, side, half] for half in range(2)] for side in range(2)]

    def fold(value):
        return jnp.sum(value.reshape(blocks, 8, cols), axis=0)

    def store_parts(which, sums):
        for at, value in enumerate(sums):
            part[which, at:at + 1, :] = jnp.sum(value, axis=0, keepdims=True)

    zero = jnp.zeros((8, cols), F32)

    packer = Packer()
    sums = [zero] * (2 * samples)
    for z in range(levels):
        values = []
        for k in range(samples):
            b = bs[k, z]
            p = prec[z] * b
            fa[pl.ds(base(k, z) + PAD, rows), :] = p
            sums[k] = sums[k] + fold(p * b)
            values.append(p)
        packer.add(z, values)
    copies = packer.send(1, fa)
    for copy in copies:
        copy.wait()
    put_rows(1, fa)

    packs = received(1)
    packer = Packer()
    for z in range(levels):
        values = []
        for k in range(samples):
            p, u = apply(1, fa, k, z, packs)
            fb[pl.ds(base(k, z) + PAD, rows), :] = u
            sums[samples + k] = sums[samples + k] + fold(u * u + ops[z] * p * p)
            values.append(u)
        packer.add(z, values)
    store_parts(0, sums)
    copies = packer.send(2, fb)
    red = reduce_start(0)
    for copy in copies:
        copy.wait()
    put_rows(2, fb)

    packs = received(2)
    packer = Packer()
    for z in range(levels):
        values = []
        for k in range(samples):
            _, q = apply(2, fb, k, z, packs)
            q = q + ops[z] * fa[pl.ds(base(k, z) + PAD, rows), :]
            w = prec[z] * q
            out_ref[k, z] = q
            ww[pl.ds(base(k, z) + PAD, rows), :] = w
            values.append(w)
        packer.add(z, values)
    copies = packer.send(3, ww)
    reduce_finish(0, red)
    gamma = [tot[0, k:k + 1, :] for k in range(samples)]
    den = [tot[0, samples + k:samples + k + 1, :] for k in range(samples)]
    alpha = [g / d for g, d in zip(gamma, den)]
    sums = [zero] * (2 * samples)
    for z in range(levels):
        for k in range(samples):
            r = bs[k, z] - alpha[k] * out_ref[k, z]
            zv = prec[z] * r
            sums[k] = sums[k] + fold(zv * r)
            fb[pl.ds(base(k, z) + PAD, rows), :] = zv
    for copy in copies:
        copy.wait()

    got = row_recv[3]
    span = samples * levels
    sample_of = lax.broadcasted_iota(jnp.int32, (span, cols), 0) // levels
    alpha_rows = jnp.zeros((span, cols), F32)
    for k in range(samples):
        alpha_rows = jnp.where(sample_of == k, alpha[k], alpha_rows)
    halo = row_recv[1] - alpha_rows * got
    fb[pl.ds(PAD - 1, span, stride=high), :] = jnp.where(is_low, 0.0, halo)
    fb[pl.ds(PAD + rows, span, stride=high), :] = jnp.where(is_low, halo, 0.0)
    lane_sample = lax.rem(lane1, per_level) // blocks
    alpha_lanes = jnp.zeros((8, cols), F32)
    for k in range(samples):
        alpha_lanes = jnp.where(lane_sample == k, alpha[k], alpha_lanes)
    packs = [
        [a - alpha_lanes * b for a, b in zip(first, second)]
        for first, second in zip(received(1), received(3))
    ]
    for z in range(levels):
        for k in range(samples):
            zv, u = apply(3, fb, k, z, packs)
            sums[samples + k] = sums[samples + k] + fold(u * u + ops[z] * zv * zv)
    store_parts(1, sums)
    red = reduce_start(1)
    reduce_finish(1, red)
    for k in range(samples):
        new = tot[1, k:k + 1, :]
        beta = new / gamma[k]
        step = new / (tot[1, samples + k:samples + k + 1, :] - beta * beta * den[k])
        p_scale = alpha[k] + step * beta
        for z in range(levels):
            at = pl.ds(base(k, z) + PAD, rows)
            out_ref[k, z] = p_scale * fa[at, :] + step * fb[at, :]


def per_device(n_lon, rs, ka, fx, fy, fz, wm, oc, ow, od):
    samples, levels, rows, cols = rs.shape
    count = oc.shape[-1]
    cell = (levels, rows, cols)
    high = rows + 2 * PAD
    field = pltpu.VMEM((samples * levels * high, cols), F32)
    group = 2 * n_lon
    coef = pltpu.VMEM(cell, F32)
    vmem = pl.BlockSpec(memory_space=pltpu.VMEM)
    return pl.pallas_call(
        functools.partial(kernel, n_lon),
        out_shape=jax.ShapeDtypeStruct(rs.shape, F32),
        in_specs=[vmem] * 9,
        out_specs=vmem,
        scratch_shapes=[
            pltpu.VMEM((levels * rows, count), jnp.bfloat16),
            pltpu.VMEM(rs.shape, F32),
            coef, coef, coef, coef, coef, coef, coef, coef,
            field, field, field,
            pltpu.VMEM((4, 2, 2, 8, cols), F32),
            pltpu.VMEM((4, 2, 2, 8, cols), F32),
            pltpu.VMEM((4, samples * levels, cols), F32),
            pltpu.VMEM((4, samples * levels, cols), F32),
            pltpu.VMEM((2, 2 * samples, cols), F32),
            pltpu.VMEM((2, group - 1, 2 * samples, cols), F32),
            pltpu.VMEM((2, 2 * samples, cols), F32),
            pltpu.SemaphoreType.DMA((4, 3)),
            pltpu.SemaphoreType.DMA((4, 3)),
            pltpu.SemaphoreType.DMA((2, group - 1)),
            pltpu.SemaphoreType.DMA((2, group - 1)),
        ],
        compiler_params=pltpu.CompilerParams(
            collective_id=0, has_side_effects=True, vmem_limit_bytes=40 * 1024 * 1024),
        cost_estimate=pl.CostEstimate(
            flops=4 * 10**9, bytes_accessed=3 * 10**6, transcendentals=0),
    )(rs, ka, fx, fy, fz, wm, oc, ow, od)


def solution(mesh):
    assert mesh.shape["lat"] == 2
    return jax.shard_map(
        functools.partial(per_device, mesh.shape["lon"]),
        mesh=mesh,
        in_specs=(
            P("grp", None, "lat", "lon"),
            P(None, "lat", "lon"),
            P(None, "lat", "lon"),
            P(None, "lat", "lon"),
            P(None, "lat", "lon"),
            P(None, "lat", "lon"),
            P("lat", "lon", None),
            P("lat", "lon", None),
            P("grp", "lat", "lon", None),
        ),
        out_specs=P("grp", None, "lat", "lon"),
        check_vma=False,
    )
```

time: 226 us -> 40.5 us (0.18)
  blocking collectives: 98.2 us -> 0 us
  other arithmetic: 46.5 us -> 0 us
  Pallas kernels: 0 us -> 31.4 us
  starting transfers between devices: 29.1 us -> 0 us
  local copies, waits for them, and re-layouts: 35.5 us -> 8.65 us
  waiting for transfers between devices: 14.9 us -> 0 us
    psum x3 -> x0, blocking collectives: 98.2 us -> none  [the longest x2 63.9 us: norm_sum(): return lax.psum(inner_sums(resid_now, zvec_now), ('lon', 'lat'))]
    scatter-add x2 -> x0, other arithmetic: 31.4 us -> none  [the longest x1 20.1 us: per_device(): shift = jnp.zeros((samples, cells), jnp.float32).at[:, flat].add(valued)....]
    pallas_call x0 -> x1, Pallas kernels: none -> 31.4 us  [per_device(): pl.pallas_call(functools.partial(kernel, n_lon), out_shape=jax.ShapeDtype...]
    ppermute x20 -> x0, starting transfers between devices: 29.1 us -> none  [the longest x10 26.6 us: padded_2(): lax.ppermute(lax.slice_in_dim(block, 0, width, axis=dim), axis, backward)]
    ppermute x20 -> x0, waiting for transfers between devices: 14.9 us -> none  [the longest x10 11.9 us: padded_2(): lax.ppermute(lax.slice_in_dim(block, block.shape[dim] - width, None, axis...]
    reshape x1 -> x0, local copies, waits for them, and re-layouts: 11.4 us -> none  [per_device(): shift = jnp.zeros((samples, cells), jnp.float32).at[:, flat].add(valued)....]
    slice x28 -> x0, local copies, waits for them, and re-layouts: 9.39 us -> none  [the longest x14 5.36 us: padded_2(): lax.slice_in_dim(block, block.shape[dim] - width, None, axis=dim)]
    ppermute x18 -> x0, local copies, waits for them, and re-layouts: 8.23 us -> none  [the longest x9 5.66 us: padded_2(): lax.ppermute(lax.slice_in_dim(block, 0, width, axis=dim), axis, backward)]
  transfers between devices with their start and end apart: 20 -> 0, of which waited for: 13 -> 0; matrix products, arithmetic and copies ran while one was open for 22% -> 0% of each run, Pallas kernels for 0% -> 0%
where the time goes in v1:
time: 40.5 us; the launch traced here: 40.1 us
  Pallas kernels  31.4 us (78%)
  local copies, waits for them, and re-layouts  8.65 us (21%)
    pallas_call x1, Pallas kernels, per_device(): pl.pallas_call(functools.partial(kernel, n_lon), out_shape=jax.ShapeDtype...  31.4 us
    unnamed x19, local copies, waits for them, and re-layouts  8.65 us

profile of v1, /device:TPU:0, one launch (start us, length us, event | category | flops | bytes accessed | tf_op | source)
XLA Modules:
  0.0 40.1 jit_solution(1259051284064578851)
XLA Ops:
  0.0 0.0 copy-start
  0.0 1.1 %copy-done = f32[4,10,32,128]{3,2,1,0:T(8,128)S(1)} copy-done((f32[4,10,32,128]{3,2,1,0:T(8,128)S(1)}, f32[4,10,32,128]{3,2,1,0:T(8,128)}, u32[]{:S(2)}) %copy-start) | copy-done | bytes 655384
  1.1 0.0 copy-start.1
  1.1 0.9 %copy-done.1 = f32[10,32,128]{2,1,0:T(8,128)S(1)} copy-done((f32[10,32,128]{2,1,0:T(8,128)S(1)}, f32[10,32,128]{2,1,0:T(8,128)}, u32[]{:S(2)}) %copy-start.1) | copy-done | bytes 163864
  2.0 0.0 copy-start.2
  2.0 0.9 %copy-done.2 = f32[10,32,128]{2,1,0:T(8,128)S(1)} copy-done((f32[10,32,128]{2,1,0:T(8,128)S(1)}, f32[10,32,128]{2,1,0:T(8,128)}, u32[]{:S(2)}) %copy-start.2) | copy-done | bytes 163864
  2.9 0.0 copy-start.3
  2.9 0.9 %copy-done.3 = f32[10,32,128]{2,1,0:T(8,128)S(1)} copy-done((f32[10,32,128]{2,1,0:T(8,128)S(1)}, f32[10,32,128]{2,1,0:T(8,128)}, u32[]{:S(2)}) %copy-start.3) | copy-done | bytes 163864
  3.8 0.0 copy-start.4
  3.8 0.9 %copy-done.4 = f32[10,32,128]{2,1,0:T(8,128)S(1)} copy-done((f32[10,32,128]{2,1,0:T(8,128)S(1)}, f32[10,32,128]{2,1,0:T(8,128)}, u32[]{:S(2)}) %copy-start.4) | copy-done | bytes 163864
  4.8 0.0 copy-start.5
  4.8 0.9 %copy-done.5 = s32[10,32,128]{2,1,0:T(8,128)S(1)} copy-done((s32[10,32,128]{2,1,0:T(8,128)S(1)}, s32[10,32,128]{2,1,0:T(8,128)}, u32[]{:S(2)}) %copy-start.5) | copy-done | bytes 163864
  5.7 0.0 copy-start.6
  5.7 0.8 %copy-done.6 = f32[4,1,1,2048]{3,2,1,0:T(1,128)S(1)} copy-done((f32[4,1,1,2048]{3,2,1,0:T(1,128)S(1)}, f32[4,1,1,2048]{3,2,1,0:T(1,128)}, u32[]{:S(2)}) %copy-start.6) | copy-done | bytes 32792
  6.4 0.0 copy-start.7
  6.4 0.7 %copy-done.7 = s32[1,1,2048]{2,1,0:T(1,128)S(1)} copy-done((s32[1,1,2048]{2,1,0:T(1,128)S(1)}, s32[1,1,2048]{2,1,0:T(1,128)}, u32[]{:S(2)}) %copy-start.7) | copy-done | bytes 8216
  7.1 0.0 copy-start.8
  7.1 0.7 %copy-done.8 = f32[1,1,2048]{2,1,0:T(1,128)S(1)} copy-done((f32[1,1,2048]{2,1,0:T(1,128)S(1)}, f32[1,1,2048]{2,1,0:T(1,128)}, u32[]{:S(2)}) %copy-start.8) | copy-done | bytes 8216
  7.8 31.4 %shard_map.91 = f32[4,10,32,128]{3,2,1,0:T(8,128)S(1)} custom-call(f32[4,10,32,128]{3,2,1,0:T(8,128)S(1)} %copy-done, f32[10,32,128]{2,1,0:T(8,128)S(1)} %copy-done.1, f32[10,32,128]{2,1,0:T(8,128)S(1)} %copy-done.2, f32[10,32,128]{2,1,0:T(8,128)S(1)} %copy-done.3, f32[10,32,128]{2,1,0:T(8,128)S(1)} %copy-done.4, s32[10,32,128]{2,1,0:T(8,128)S(1)} %copy-done.5, ...), custom_call_target="tpu_custom_call" | custom-call | flops 4000000000 | bytes 3000000 | tf_op jit(solution)/shard_map/pallas_call | solution.py:325
  39.2 0.8 %copy.11 = f32[4,10,32,128]{3,2,1,0:T(8,128)} copy(f32[4,10,32,128]{3,2,1,0:T(8,128)S(1)} %shard_map.91) | data formatting | bytes 1310720
Async XLA Ops:
  0.0 1.1 %copy-start = (f32[4,10,32,128]{3,2,1,0:T(8,128)S(1)}, f32[4,10,32,128]{3,2,1,0:T(8,128)}, u32[]{:S(2)}) copy-start(f32[4,10,32,128]{3,2,1,0:T(8,128)} %rs_ref.1) | copy-start | bytes 1966084
  1.1 0.9 %copy-start.1 = (f32[10,32,128]{2,1,0:T(8,128)S(1)}, f32[10,32,128]{2,1,0:T(8,128)}, u32[]{:S(2)}) copy-start(f32[10,32,128]{2,1,0:T(8,128)} %ka_ref.1) | copy-start | bytes 491524
  2.0 0.9 %copy-start.2 = (f32[10,32,128]{2,1,0:T(8,128)S(1)}, f32[10,32,128]{2,1,0:T(8,128)}, u32[]{:S(2)}) copy-start(f32[10,32,128]{2,1,0:T(8,128)} %fx_ref.1) | copy-start | bytes 491524
  2.9 0.9 %copy-start.3 = (f32[10,32,128]{2,1,0:T(8,128)S(1)}, f32[10,32,128]{2,1,0:T(8,128)}, u32[]{:S(2)}) copy-start(f32[10,32,128]{2,1,0:T(8,128)} %fy_ref.1) | copy-start | bytes 491524
  3.8 0.9 %copy-start.4 = (f32[10,32,128]{2,1,0:T(8,128)S(1)}, f32[10,32,128]{2,1,0:T(8,128)}, u32[]{:S(2)}) copy-start(f32[10,32,128]{2,1,0:T(8,128)} %fz_ref.1) | copy-start | bytes 491524
  4.8 0.9 %copy-start.5 = (s32[10,32,128]{2,1,0:T(8,128)S(1)}, s32[10,32,128]{2,1,0:T(8,128)}, u32[]{:S(2)}) copy-start(s32[10,32,128]{2,1,0:T(8,128)} %wm_ref.1) | copy-start | bytes 491524
  5.7 0.8 %copy-start.6 = (f32[4,1,1,2048]{3,2,1,0:T(1,128)S(1)}, f32[4,1,1,2048]{3,2,1,0:T(1,128)}, u32[]{:S(2)}) copy-start(f32[4,1,1,2048]{3,2,1,0:T(1,128)} %od_ref.1) | copy-start | bytes 98308
  6.4 0.7 %copy-start.7 = (s32[1,1,2048]{2,1,0:T(1,128)S(1)}, s32[1,1,2048]{2,1,0:T(1,128)}, u32[]{:S(2)}) copy-start(s32[1,1,2048]{2,1,0:T(1,128)} %oc_ref.1) | copy-start | bytes 24580
  7.1 0.7 %copy-start.8 = (f32[1,1,2048]{2,1,0:T(1,128)S(1)}, f32[1,1,2048]{2,1,0:T(1,128)}, u32[]{:S(2)}) copy-start(f32[1,1,2048]{2,1,0:T(1,128)} %ow_ref.1) | copy-start | bytes 24580

commit v2 on v1

--- a/solution.py
+++ b/solution.py
@@ -13,10 +13,11 @@
 
 
 def kernel(
-    n_lon, rs_ref, ka_ref, fx_ref, fy_ref, fz_ref, wm_ref, oc_ref, ow_ref, od_ref, out_ref,
+    n_lon, rs_in, ka_in, fx_in, fy_in, fz_in, wm_in, oc_in, ow_in, od_in, out_ref,
+    rs_ref, ka_ref, fx_ref, fy_ref, fz_ref, wm_ref, oc_ref, ow_ref, od_ref,
     row_hot, bs, ops, prec, dg, cx, cxl, cy, cyu, cz, fa, fb, ww,
     col_send, col_recv, row_send, row_recv, part, slots, tot,
-    send_sem, recv_sem, red_send, red_recv,
+    send_sem, recv_sem, red_send, red_recv, load_sem,
 ):
     samples, levels, rows, cols = rs_ref.shape
     blocks = rows // 8
@@ -33,6 +34,14 @@
         other = lax.rem(me + step, group)
         return (grp, other // 2, lax.rem(other, 2))
 
+    pairs = (
+        (wm_in, wm_ref), (fx_in, fx_ref), (fy_in, fy_ref), (oc_in, oc_ref), (ow_in, ow_ref),
+        (od_in, od_ref), (rs_in, rs_ref), (ka_in, ka_ref), (fz_in, fz_ref))
+    loads = [
+        pltpu.make_async_copy(source, here, load_sem.at[at])
+        for at, (source, here) in enumerate(pairs)]
+    for load in loads:
+        load.start()
     barrier = pltpu.get_barrier_semaphore()
     for step in range(1, group):
         pl.semaphore_signal(barrier, inc=1, device_id=peer(step), device_id_type=MESH)
@@ -42,7 +51,6 @@
     lane32 = lax.broadcasted_iota(jnp.int32, (rows, cols), 1)
     row32 = lax.broadcasted_iota(jnp.int32, (rows, cols), 0)
     first_lane, last_lane = lane32 == 0, lane32 == cols - 1
-    edge = jnp.where(is_low, rows - 1, 0)
 
     def exchange(slot):
         copies = []
@@ -77,6 +85,9 @@
             total = total + slots[which, step]
         tot[which] = jnp.broadcast_to(jnp.sum(total, axis=1, keepdims=True), total.shape)
 
+    for load in loads[:3]:
+        load.wait()
+
     to_right = jnp.zeros((8, cols), F32)
     to_left = jnp.zeros((8, cols), F32)
     for z in range(levels):
@@ -100,6 +111,9 @@
 
     pl.semaphore_wait(barrier, group - 1)
     copies = exchange(0)
+
+    for load in loads[3:]:
+        load.wait()
 
     count = oc_ref.shape[-1]
     cells = oc_ref[0]
@@ -322,12 +336,14 @@
     group = 2 * n_lon
     coef = pltpu.VMEM(cell, F32)
     vmem = pl.BlockSpec(memory_space=pltpu.VMEM)
+    hbm = pl.BlockSpec(memory_space=pltpu.HBM)
+    args = (rs, ka, fx, fy, fz, wm, oc, ow, od)
     return pl.pallas_call(
         functools.partial(kernel, n_lon),
         out_shape=jax.ShapeDtypeStruct(rs.shape, F32),
-        in_specs=[vmem] * 9,
+        in_specs=[hbm] * len(args),
         out_specs=vmem,
-        scratch_shapes=[
+        scratch_shapes=[pltpu.VMEM(a.shape, a.dtype) for a in args] + [
             pltpu.VMEM((levels * rows, count), jnp.bfloat16),
             pltpu.VMEM(rs.shape, F32),
             coef, coef, coef, coef, coef, coef, coef, coef,
@@ -343,12 +359,13 @@
             pltpu.SemaphoreType.DMA((4, 3)),
             pltpu.SemaphoreType.DMA((2, group - 1)),
             pltpu.SemaphoreType.DMA((2, group - 1)),
+            pltpu.SemaphoreType.DMA((len(args),)),
         ],
         compiler_params=pltpu.CompilerParams(
-            collective_id=0, has_side_effects=True, vmem_limit_bytes=40 * 1024 * 1024),
+            collective_id=0, has_side_effects=True, vmem_limit_bytes=60 * 1024 * 1024),
         cost_estimate=pl.CostEstimate(
             flops=4 * 10**9, bytes_accessed=3 * 10**6, transcendentals=0),
-    )(rs, ka, fx, fy, fz, wm, oc, ow, od)
+    )(*args)
 
 
 def solution(mesh):

time: 40.5 us -> 35.2 us (0.87)
  local copies, waits for them, and re-layouts: 8.65 us -> 1.97 us
  Pallas kernels: 31.4 us -> 33.1 us
    unnamed x19 -> x1, local copies, waits for them, and re-layouts: 8.65 us -> 1.97 us
    pallas_call x1, Pallas kernels: 31.4 us -> 33.1 us  [per_device(): pl.pallas_call(functools.partial(kernel, n_lon), out_shape=jax.ShapeDtype...]
where the time goes in v2:
time: 35.2 us; the launch traced here: 35.1 us
  Pallas kernels  33.1 us (94%)
  local copies, waits for them, and re-layouts  1.97 us (6%)
    pallas_call x1, Pallas kernels, per_device(): pl.pallas_call(functools.partial(kernel, n_lon), out_shape=jax.ShapeDtype...  33.1 us
    unnamed x1, local copies, waits for them, and re-layouts  1.97 us

profile of v2, /device:TPU:0, one launch (start us, length us, event | category | flops | bytes accessed | tf_op | source)
XLA Modules:
  0.0 35.1 jit_solution(8110629357241454046)
XLA Ops:
  0.0 33.1 %shard_map.91 = f32[4,10,32,128]{3,2,1,0:T(8,128)} custom-call(f32[4,10,32,128]{3,2,1,0:T(8,128)} %rs_in.1, f32[10,32,128]{2,1,0:T(8,128)} %ka_in.1, f32[10,32,128]{2,1,0:T(8,128)} %fx_in.1, f32[10,32,128]{2,1,0:T(8,128)} %fy_in.1, f32[10,32,128]{2,1,0:T(8,128)} %fz_in.1, s32[10,32,128]{2,1,0:T(8,128)} %wm_in.1, s32[1,1,2048]{2,1,0:T(1,128)} %oc_in.1, ...), custom_call_target="tpu_custom_call" | custom-call | flops 4000000000 | bytes 3000000 | tf_op jit(solution)/shard_map/pallas_call | solution.py:341
  33.1 2.0 %copy.11 = f32[4,10,32,128]{3,2,1,0:T(8,128)} copy(f32[4,10,32,128]{3,2,1,0:T(8,128)} %shard_map.91) | data formatting | bytes 1310720

commit v3 on v2

--- a/solution.py
+++ b/solution.py
@@ -13,11 +13,11 @@
 
 
 def kernel(
-    n_lon, rs_in, ka_in, fx_in, fy_in, fz_in, wm_in, oc_in, ow_in, od_in, out_ref,
+    n_lon, rs_in, ka_in, fx_in, fy_in, fz_in, wm_in, oc_in, ow_in, od_in, out,
     rs_ref, ka_ref, fx_ref, fy_ref, fz_ref, wm_ref, oc_ref, ow_ref, od_ref,
-    row_hot, bs, ops, prec, dg, cx, cxl, cy, cyu, cz, fa, fb, ww,
+    out_ref, row_hot, bs, ops, prec, dg, cx, cxl, cy, cyu, cz, fa, fb, ww,
     col_send, col_recv, row_send, row_recv, part, slots, tot,
-    send_sem, recv_sem, red_send, red_recv, load_sem,
+    send_sem, recv_sem, red_send, red_recv, load_sem, out_sem,
 ):
     samples, levels, rows, cols = rs_ref.shape
     blocks = rows // 8
@@ -63,7 +63,7 @@
             src_ref=row_send.at[slot], dst_ref=row_recv.at[slot],
             send_sem=send_sem.at[slot, 2], recv_sem=recv_sem.at[slot, 2],
             device_id=(grp, lon, 1 - lat), device_id_type=MESH))
-        for copy in copies:
+        for copy in (copies[2], copies[0], copies[1]):
             copy.start()
         return copies
 
@@ -259,8 +259,8 @@
             sums[samples + k] = sums[samples + k] + fold(u * u + ops[z] * p * p)
             values.append(u)
         packer.add(z, values)
+    copies = packer.send(2, fb)
     store_parts(0, sums)
-    copies = packer.send(2, fb)
     red = reduce_start(0)
     for copy in copies:
         copy.wait()
@@ -317,6 +317,8 @@
     store_parts(1, sums)
     red = reduce_start(1)
     reduce_finish(1, red)
+    stores = [
+        pltpu.make_async_copy(out_ref.at[k], out.at[k], out_sem.at[k]) for k in range(samples)]
     for k in range(samples):
         new = tot[1, k:k + 1, :]
         beta = new / gamma[k]
@@ -325,6 +327,9 @@
         for z in range(levels):
             at = pl.ds(base(k, z) + PAD, rows)
             out_ref[k, z] = p_scale * fa[at, :] + step * fb[at, :]
+        stores[k].start()
+    for store in stores:
+        store.wait()
 
 
 def per_device(n_lon, rs, ka, fx, fy, fz, wm, oc, ow, od):
@@ -335,15 +340,15 @@
     field = pltpu.VMEM((samples * levels * high, cols), F32)
     group = 2 * n_lon
     coef = pltpu.VMEM(cell, F32)
-    vmem = pl.BlockSpec(memory_space=pltpu.VMEM)
     hbm = pl.BlockSpec(memory_space=pltpu.HBM)
     args = (rs, ka, fx, fy, fz, wm, oc, ow, od)
     return pl.pallas_call(
         functools.partial(kernel, n_lon),
         out_shape=jax.ShapeDtypeStruct(rs.shape, F32),
         in_specs=[hbm] * len(args),
-        out_specs=vmem,
+        out_specs=hbm,
         scratch_shapes=[pltpu.VMEM(a.shape, a.dtype) for a in args] + [
+            pltpu.VMEM(rs.shape, F32),
             pltpu.VMEM((levels * rows, count), jnp.bfloat16),
             pltpu.VMEM(rs.shape, F32),
             coef, coef, coef, coef, coef, coef, coef, coef,
@@ -360,6 +365,7 @@
             pltpu.SemaphoreType.DMA((2, group - 1)),
             pltpu.SemaphoreType.DMA((2, group - 1)),
             pltpu.SemaphoreType.DMA((len(args),)),
+            pltpu.SemaphoreType.DMA((samples,)),
         ],
         compiler_params=pltpu.CompilerParams(
             collective_id=0, has_side_effects=True, vmem_limit_bytes=60 * 1024 * 1024),

time: 35.2 us -> 35.2 us (level)
  no operation moved by 1% of the time
where the time goes in v3:
time: 35.2 us; the launch traced here: 35.1 us
  Pallas kernels  33.1 us (94%)
  local copies, waits for them, and re-layouts  1.97 us (6%)
    pallas_call x1, Pallas kernels, per_device(): pl.pallas_call(functools.partial(kernel, n_lon), out_shape=jax.ShapeDtype...  33.1 us
    unnamed x1, local copies, waits for them, and re-layouts  1.97 us

profile of v3, /device:TPU:0, one launch (start us, length us, event | category | flops | bytes accessed | tf_op | source)
XLA Modules:
  0.0 35.1 jit_solution(14450068474499886170)
XLA Ops:
  0.0 33.1 %shard_map.91 = f32[4,10,32,128]{3,2,1,0:T(8,128)} custom-call(f32[4,10,32,128]{3,2,1,0:T(8,128)} %rs_in.1, f32[10,32,128]{2,1,0:T(8,128)} %ka_in.1, f32[10,32,128]{2,1,0:T(8,128)} %fx_in.1, f32[10,32,128]{2,1,0:T(8,128)} %fy_in.1, f32[10,32,128]{2,1,0:T(8,128)} %fz_in.1, s32[10,32,128]{2,1,0:T(8,128)} %wm_in.1, s32[1,1,2048]{2,1,0:T(1,128)} %oc_in.1, ...), custom_call_target="tpu_custom_call" | custom-call | flops 4000000000 | bytes 3000000 | tf_op jit(solution)/shard_map/pallas_call | solution.py:345
  33.1 2.0 %copy.11 = f32[4,10,32,128]{3,2,1,0:T(8,128)} copy(f32[4,10,32,128]{3,2,1,0:T(8,128)} %shard_map.91) | data formatting | bytes 1310720

commit v4 on v3

--- a/solution.py
+++ b/solution.py
@@ -15,7 +15,7 @@
 def kernel(
     n_lon, rs_in, ka_in, fx_in, fy_in, fz_in, wm_in, oc_in, ow_in, od_in, out,
     rs_ref, ka_ref, fx_ref, fy_ref, fz_ref, wm_ref, oc_ref, ow_ref, od_ref,
-    out_ref, row_hot, bs, ops, prec, dg, cx, cxl, cy, cyu, cz, fa, fb, ww,
+    out_ref, row_hot, bs, ops, prec, dg, cx, cxl, cy, cyu, cz, ce, fa, fb, ww,
     col_send, col_recv, row_send, row_recv, part, slots, tot,
     send_sem, recv_sem, red_send, red_recv, load_sem, out_sem,
 ):
@@ -165,8 +165,11 @@
         scaled = mask * diag + (1.0 - mask)
         dg[z] = scaled
         prec[z] = 1.0 / (scaled * scaled + ops[z])
-        cx[z] = flux_x * mask * m_right
-        cxl[z] = fx_left * mask * m_left
+        east = flux_x * mask * m_right
+        west = fx_left * mask * m_left
+        cx[z] = jnp.where(last_lane, 0.0, east)
+        cxl[z] = jnp.where(first_lane, 0.0, west)
+        ce[z] = jnp.where(first_lane, west, jnp.where(last_lane, east, 0.0))
         cy[z] = flux_y * mask * m_down
         cyu[z] = fy_up * mask * m_up
         if z + 1 < levels:
@@ -206,20 +209,22 @@
         field[pl.ds(PAD - 1, samples * levels, stride=high), :] = jnp.where(is_low, 0.0, got)
         field[pl.ds(PAD + rows, samples * levels, stride=high), :] = jnp.where(is_low, got, 0.0)
 
-    def apply(slot, field, k, z, packs):
+    def inside(field, k, z):
         at = base(k, z) + PAD
         here = field[pl.ds(at, rows), :]
-        up = field[pl.ds(at - 1, rows), :]
-        down = field[pl.ds(at + 1, rows), :]
-        half, lane = z // per_vreg, (z % per_vreg) * per_level + k * blocks
-        west = jnp.where(first_lane, column(packs[0][half], lane), pltpu.roll(here, 1, 1))
-        east = jnp.where(last_lane, column(packs[1][half], lane), pltpu.roll(here, cols - 1, 1))
-        total = dg[z] * here - cx[z] * east - cxl[z] * west - cy[z] * down - cyu[z] * up
+        total = dg[z] * here - cx[z] * pltpu.roll(here, cols - 1, 1) - cxl[z] * pltpu.roll(here, 1, 1)
         if z > 0:
             total = total - cz[z - 1] * field[pl.ds(at - high, rows), :]
         if z + 1 < levels:
             total = total - cz[z] * field[pl.ds(at + high, rows), :]
-        return here, total
+        return total
+
+    def finish(total, field, k, z, packs):
+        at = base(k, z) + PAD
+        half, lane = z // per_vreg, (z % per_vreg) * per_level + k * blocks
+        side = jnp.where(first_lane, column(packs[0][half], lane), column(packs[1][half], lane))
+        return (total - cy[z] * field[pl.ds(at + 1, rows), :]
+                - cyu[z] * field[pl.ds(at - 1, rows), :] - ce[z] * side)
 
     def received(slot):
         return [[col_recv[slot, side, half] for half in range(2)] for side in range(2)]
@@ -245,6 +250,9 @@
             values.append(p)
         packer.add(z, values)
     copies = packer.send(1, fa)
+    for z in range(levels):
+        for k in range(samples):
+            fb[pl.ds(base(k, z) + PAD, rows), :] = inside(fa, k, z)
     for copy in copies:
         copy.wait()
     put_rows(1, fa)
@@ -254,14 +262,20 @@
     for z in range(levels):
         values = []
         for k in range(samples):
-            p, u = apply(1, fa, k, z, packs)
-            fb[pl.ds(base(k, z) + PAD, rows), :] = u
+            at = pl.ds(base(k, z) + PAD, rows)
+            p = fa[at, :]
+            u = finish(fb[at, :], fa, k, z, packs)
+            fb[at, :] = u
             sums[samples + k] = sums[samples + k] + fold(u * u + ops[z] * p * p)
             values.append(u)
         packer.add(z, values)
     copies = packer.send(2, fb)
     store_parts(0, sums)
     red = reduce_start(0)
+    for z in range(levels):
+        for k in range(samples):
+            p = fa[pl.ds(base(k, z) + PAD, rows), :]
+            out_ref[k, z] = inside(fb, k, z) + ops[z] * p
     for copy in copies:
         copy.wait()
     put_rows(2, fb)
@@ -271,8 +285,7 @@
     for z in range(levels):
         values = []
         for k in range(samples):
-            _, q = apply(2, fb, k, z, packs)
-            q = q + ops[z] * fa[pl.ds(base(k, z) + PAD, rows), :]
+            q = finish(out_ref[k, z], fb, k, z, packs)
             w = prec[z] * q
             out_ref[k, z] = q
             ww[pl.ds(base(k, z) + PAD, rows), :] = w
@@ -290,6 +303,9 @@
             zv = prec[z] * r
             sums[k] = sums[k] + fold(zv * r)
             fb[pl.ds(base(k, z) + PAD, rows), :] = zv
+    for z in range(levels):
+        for k in range(samples):
+            ww[pl.ds(base(k, z) + PAD, rows), :] = inside(fb, k, z)
     for copy in copies:
         copy.wait()
 
@@ -312,7 +328,9 @@
     ]
     for z in range(levels):
         for k in range(samples):
-            zv, u = apply(3, fb, k, z, packs)
+            at = pl.ds(base(k, z) + PAD, rows)
+            zv = fb[at, :]
+            u = finish(ww[at, :], fb, k, z, packs)
             sums[samples + k] = sums[samples + k] + fold(u * u + ops[z] * zv * zv)
     store_parts(1, sums)
     red = reduce_start(1)
@@ -351,7 +369,7 @@
             pltpu.VMEM(rs.shape, F32),
             pltpu.VMEM((levels * rows, count), jnp.bfloat16),
             pltpu.VMEM(rs.shape, F32),
-            coef, coef, coef, coef, coef, coef, coef, coef,
+            coef, coef, coef, coef, coef, coef, coef, coef, coef,
             field, field, field,
             pltpu.VMEM((4, 2, 2, 8, cols), F32),
             pltpu.VMEM((4, 2, 2, 8, cols), F32),

time: 35.2 us -> 33.6 us (0.955)
  Pallas kernels: 33.1 us -> 31.4 us
    pallas_call x1, Pallas kernels: 33.1 us -> 31.4 us  [per_device(): pl.pallas_call(functools.partial(kernel, n_lon), out_shape=jax.ShapeDtype...]
where the time goes in v4:
time: 33.6 us; the launch traced here: 33.4 us
  Pallas kernels  31.4 us (93%)
  local copies, waits for them, and re-layouts  1.97 us (6%)
    pallas_call x1, Pallas kernels, per_device(): pl.pallas_call(functools.partial(kernel, n_lon), out_shape=jax.ShapeDtype...  31.4 us
    unnamed x1, local copies, waits for them, and re-layouts  1.97 us

profile of v4, /device:TPU:0, one launch (start us, length us, event | category | flops | bytes accessed | tf_op | source)
XLA Modules:
  0.0 33.4 jit_solution(7804447767815526090)
XLA Ops:
  0.0 31.4 %shard_map.91 = f32[4,10,32,128]{3,2,1,0:T(8,128)} custom-call(f32[4,10,32,128]{3,2,1,0:T(8,128)} %rs_in.1, f32[10,32,128]{2,1,0:T(8,128)} %ka_in.1, f32[10,32,128]{2,1,0:T(8,128)} %fx_in.1, f32[10,32,128]{2,1,0:T(8,128)} %fy_in.1, f32[10,32,128]{2,1,0:T(8,128)} %fz_in.1, s32[10,32,128]{2,1,0:T(8,128)} %wm_in.1, s32[1,1,2048]{2,1,0:T(1,128)} %oc_in.1, ...), custom_call_target="tpu_custom_call" | custom-call | flops 4000000000 | bytes 3000000 | tf_op jit(solution)/shard_map/pallas_call | solution.py:363
  31.4 2.0 %copy.11 = f32[4,10,32,128]{3,2,1,0:T(8,128)} copy(f32[4,10,32,128]{3,2,1,0:T(8,128)} %shard_map.91) | data formatting | bytes 1310720
